TPU v7x, 128 devices: a whole 4x4x4 slice. The times are simulated.
128 devices in a mesh: dp: 32 (over x, z, core), ctx: 4 (over y).
Axes of the slice: x: 4, y: 4, z: 4, core: 2. Of those that a mesh axis runs over, the one named last changes fastest.
Arguments:
- activations: bfloat16 [32, 512, 1152], P('dp', 'ctx'), may hold values from -6 to 6
- cotangent: bfloat16 [32, 512, 1152], P('dp', 'ctx'), may hold values from -6 to 6
- segments: int32 [32, 512], P('dp'), may hold values from 0 to 4, as said below
- in_gain: bfloat16 [1152], P(('dp', 'ctx')), may hold values from -0.5 to 0.5
- query_gain: bfloat16 [256], P(('dp', 'ctx')), may hold values from -0.5 to 0.5
- key_gain: bfloat16 [256], P(('dp', 'ctx')), may hold values from -0.5 to 0.5
- post_attn_gain: bfloat16 [1152], P(('dp', 'ctx')), may hold values from -0.5 to 0.5
- pre_ff_gain: bfloat16 [1152], P(('dp', 'ctx')), may hold values from -0.5 to 0.5
- post_ff_gain: bfloat16 [1152], P(('dp', 'ctx')), may hold values from -0.5 to 0.5
- w_query: bfloat16 [1152, 1024], P(('dp', 'ctx')), may hold values from -0.1875 to 0.1875
- w_key: bfloat16 [1152, 256], P(('dp', 'ctx')), may hold values from -0.1875 to 0.1875
- w_value: bfloat16 [1152, 256], P(('dp', 'ctx')), may hold values from -0.1875 to 0.1875
- w_out: bfloat16 [1024, 1152], P(('dp', 'ctx')), may hold values from -0.1875 to 0.1875
- w_gate: bfloat16 [1152, 6912], P(('dp', 'ctx')), may hold values from -0.1875 to 0.1875
- w_up: bfloat16 [1152, 6912], P(('dp', 'ctx')), may hold values from -0.1875 to 0.1875
- w_down: bfloat16 [6912, 1152], P(('dp', 'ctx')), may hold values from -0.078125 to 0.078125
Outputs:
- output: bfloat16 [32, 512, 1152], P('dp', 'ctx')
- input_grad: float32 [32, 512, 1152], P('dp', 'ctx')
- in_gain_grad: float32 [1152], P(('dp', 'ctx'))
- query_gain_grad: float32 [256], P(('dp', 'ctx'))
- key_gain_grad: float32 [256], P(('dp', 'ctx'))
- post_attn_gain_grad: float32 [1152], P(('dp', 'ctx'))
- pre_ff_gain_grad: float32 [1152], P(('dp', 'ctx'))
- post_ff_gain_grad: float32 [1152], P(('dp', 'ctx'))
- w_query_grad: float32 [1152, 1024], P(('dp', 'ctx'))
- w_key_grad: float32 [1152, 256], P(('dp', 'ctx'))
- w_value_grad: float32 [1152, 256], P(('dp', 'ctx'))
- w_out_grad: float32 [1024, 1152], P(('dp', 'ctx'))
- w_gate_grad: float32 [1152, 6912], P(('dp', 'ctx'))
- w_up_grad: float32 [1152, 6912], P(('dp', 'ctx'))
- w_down_grad: float32 [6912, 1152], P(('dp', 'ctx'))
Inputs may be any that keep to these rules, and one draw needn't show every extreme that they name: `segments`: segment numbers never fall along a sequence and may skip values; in every sequence one document begins within the first 64 tokens and ends within the last 64 tokens.
All inputs are finite; a program needn't handle non-finite values.
Results may differ from a plain program's by a relative error of at most 0.035.
Values may be sent and summed in bfloat16 or wider, within the bound.
No kernel may reach another device: no remote copies, remote signals or barrier semaphores. Data moves between devices by JAX's collectives and lax.ppermute only.
A program may use at most 256 MiB of HBM per device.

v0:
```python
import math

import jax
import jax.numpy as jnp
from jax import lax
from jax.sharding import Mesh
from jax.sharding import PartitionSpec as P

norm_eps = 1e-06
rope_base = 1000000.0
score_scale = 0.0625
far_below = -1e30
f32 = jnp.float32
bf16 = jnp.bfloat16


def rms_norm(values, gain):
    factor = lax.rsqrt(jnp.mean(values * values, axis=-1, keepdims=True) + norm_eps)
    return values * factor * (1.0 + gain)


def rotate(values, cosine, sine):
    half_dim = values.shape[-1] // 2
    first_half = values[..., :half_dim]
    second_half = values[..., half_dim:]
    return jnp.concatenate(
        [first_half * cosine - second_half * sine, second_half * cosine + first_half * sine],
        axis=-1,
    )


def rope_tables(positions, head_dim):
    freq_index = jnp.arange(head_dim // 2, dtype=f32)
    inverse = jnp.exp(freq_index * (-2.0 / head_dim) * math.log(rope_base))
    angles = positions.astype(f32)[:, None] * inverse[None, :]
    return (jnp.cos(angles), jnp.sin(angles))


def gated_unit(gate_pre, up_pre):
    return jax.nn.gelu(gate_pre, approximate=True) * up_pre


def contract(left, right, left_dim, right_dim, kind=f32):
    return lax.dot_general(
        left, right, (((left_dim,), (right_dim,)), ((), ())), preferred_element_type=kind
    )


def from_ahead(block, step, axis="y"):
    size = lax.axis_size(axis)
    return lax.ppermute(block, axis, [(i, (i - step) % size) for i in range(size)])


def to_ahead(block, step, axis="y"):
    size = lax.axis_size(axis)
    return lax.ppermute(block, axis, [(i, (i + step) % size) for i in range(size)])


def gather_ahead(block, axis="y"):
    size = lax.axis_size(axis)
    return jnp.concatenate([block] + [from_ahead(block, s, axis) for s in range(1, size)], axis=0)


def sum_ahead(terms, axis="y"):
    arrived = [to_ahead(terms[s].astype(bf16), s, axis) for s in range(1, len(terms))]
    total = terms[0].astype(f32)
    for item in arrived:
        total = total + item.astype(f32)
    return total


def swap(pieces, axis):
    size = lax.axis_size(axis)
    me = lax.axis_index(axis)
    arrived = [lax.dynamic_index_in_dim(pieces, me, 0, keepdims=False)]
    for s in range(1, size):
        item = lax.dynamic_index_in_dim(pieces, (me + s) % size, 0, keepdims=False)
        arrived.append(to_ahead(item, s, axis))
    return by_sender(arrived, axis)


def by_sender(arrived, axis):
    size = lax.axis_size(axis)
    me = lax.axis_index(axis)
    result = []
    for c in range(size):
        item = arrived[0]
        for s in range(1, size):
            item = jnp.where((me - c) % size == s, arrived[s], item)
        result.append(item)
    return jnp.stack(result)


def gather_axis(block, axis, dim):
    size = lax.axis_size(axis)
    me = lax.axis_index(axis)
    arrived = [block] + [to_ahead(block, s, axis) for s in range(1, size)]
    result = jnp.zeros(block.shape[:dim] + (size,) + block.shape[dim:], block.dtype)
    for s in range(size):
        item = jnp.expand_dims(arrived[s], dim)
        result = lax.dynamic_update_slice_in_dim(result, item, (me - s) % size, dim)
    return result


def reduce_axis(terms, axis, dim):
    size = lax.axis_size(axis)
    me = lax.axis_index(axis)
    total = lax.dynamic_index_in_dim(terms, me, dim, keepdims=False).astype(f32)
    arrived = [
        to_ahead(lax.dynamic_index_in_dim(terms, (me + s) % size, dim, keepdims=False), s, axis)
        for s in range(1, size)
    ]
    for item in arrived:
        total = total + item.astype(f32)
    return total.astype(bf16)


def side_by_side(items, width):
    total, first = None, 0
    for item in items:
        last = width - first - item.shape[-1]
        placed = jnp.pad(item, ((0, 0),) * (item.ndim - 1) + ((first, last),))
        total = placed if total is None else total + placed
        first += item.shape[-1]
    return total


def gather_blocks(block, axis):
    size = lax.axis_size(axis)
    return by_sender([block] + [to_ahead(block, s, axis) for s in range(1, size)], axis)


def gather_team(block):
    return gather_ahead(gather_ahead(block, "y"), "core")


def sum_team(term, tokens):
    half = term.shape[0] // 2
    term = sum_ahead([term[:half], term[half:]], "core")
    return sum_ahead([term[i : i + tokens] for i in range(0, half, tokens)], "y")


def down_routes(teams, members):
    here, before = [], []
    for member in range(members):
        for block in range(teams):
            owner = member * teams + block
            here.append((owner, block * members + member))
            if block > 0:
                before.append((owner, (block - 1) * members + member))
    return here, before


def local(
    activations,
    cotangent,
    segments,
    in_gain,
    query_gain,
    key_gain,
    post_attn_gain,
    pre_ff_gain,
    post_ff_gain,
    w_query,
    w_key,
    w_value,
    w_out,
    w_gate,
    w_up,
    w_down,
):
    all_axes = ("x", "z", "core", "y")
    teams = lax.axis_size("x") * lax.axis_size("z")
    inner = lax.axis_size("y")
    cores = lax.axis_size("core")
    members = inner * cores
    me = lax.axis_index("y")
    team = lax.axis_index("x") * lax.axis_size("z") + lax.axis_index("z")
    flat = team * members + lax.axis_index("core") * inner + me
    rows = w_query.shape[0]
    model = w_down.shape[1]
    query_cols = w_query.shape[1]
    head_dim = w_key.shape[1]
    heads = query_cols // head_dim
    qkv_cols = query_cols + 2 * head_dim
    out_rows = w_out.shape[0]
    team_rows = members * rows
    part = w_gate.shape[1] // members
    wide = -(-part // 128) * 128
    down_rows = w_down.shape[0]
    down_wide = wide // teams
    down_shift = down_wide - down_rows

    half_qkv = qkv_cols // 2
    half_out = -(-model // 256) * 128
    half = half_qkv + half_out

    def halves(qkv_block, out_block):
        out_block = jnp.pad(out_block, ((0, 0),) * (out_block.ndim - 1) + ((0, 2 * half_out - model),))
        return jnp.stack(
            [
                jnp.concatenate(
                    [
                        qkv_block[..., c * half_qkv : (c + 1) * half_qkv],
                        out_block[..., c * half_out : (c + 1) * half_out],
                    ],
                    axis=-1,
                )
                for c in range(cores)
            ]
        )

    gains = (in_gain, query_gain, key_gain, post_attn_gain, pre_ff_gain, post_ff_gain)
    gain_row = side_by_side(gains, model)[None]
    attn_rows = halves(
        jnp.concatenate([w_query, w_key, w_value], axis=1),
        jnp.concatenate([w_out, gain_row], axis=0),
    )
    attn_rows = gather_blocks(attn_rows, "y").transpose(1, 0, 2, 3)
    attn_rows = swap(attn_rows, "core").reshape(members, rows, half)
    attn_shard = jnp.concatenate(
        [
            attn_rows[:, :, :half_qkv].reshape(team_rows, half_qkv),
            jnp.concatenate(
                [
                    attn_rows[:, :out_rows, half_qkv:].reshape(members * out_rows, half_out),
                    attn_rows[:, out_rows, half_qkv:],
                ],
                axis=0,
            ),
        ],
        axis=1,
    )
    def columns(weight):
        pieces = weight.reshape(rows, members, part)
        return jnp.pad(pieces, ((0, 0), (0, 0), (0, wide - part)))

    both = jnp.concatenate([columns(w_gate), columns(w_up)], axis=2).transpose(1, 0, 2)
    both = both.reshape(cores, inner, rows, 2 * wide)
    by_y = swap(both.transpose(1, 2, 0, 3).reshape(inner, rows, cores * 2 * wide), "y")
    by_core = by_y.reshape(inner, rows, cores, 2 * wide).transpose(2, 0, 1, 3)
    by_member = swap(by_core, "core").reshape(team_rows, 2 * wide)
    here, before = down_routes(teams, members)
    down_two = jnp.concatenate(
        [lax.ppermute(w_down, all_axes, here), lax.ppermute(w_down, all_axes, before)], axis=0
    )
    down_part = lax.dynamic_slice_in_dim(down_two, down_shift * team, down_wide, 0)
    shard = jnp.concatenate(
        [by_member, jnp.pad(down_part, ((0, team_rows - down_wide), (0, 0)))],
        axis=1,
    )
    full = lax.all_gather(shard, ("x", "z"), axis=0, tiled=True)
    attn_shard, _ = lax.optimization_barrier((attn_shard, shard))
    full_both = full[:, : 2 * wide]
    full_down = full.reshape(teams, team_rows, -1)[:, :down_wide, 2 * wide :].reshape(wide, model)

    left = gather_axis(gather_axis(attn_shard[:, :half_qkv], "x", 0), "z", 1)
    right = gather_axis(gather_axis(attn_shard[:, half_qkv:], "z", 0), "x", 0)
    left = by_sender([left, to_ahead(left, 1, "core")], "core")
    right = by_sender([right, to_ahead(right, 1, "core")], "core")
    right = right.reshape(cores, teams, team_rows, half_out)
    full_qkv = jnp.concatenate(
        [left[c].reshape(model, half_qkv) for c in range(cores)], axis=1
    )
    full_out = jnp.concatenate(
        [
            right[c, :, : members * out_rows].reshape(query_cols, half_out)
            for c in range(cores)
        ],
        axis=1,
    )[:, :model]
    gain_all = right[0, :, members * out_rows :, :128].astype(f32)
    full_gains = []
    first = 0
    for item in gains:
        size = item.shape[0]
        full_gains.append(gain_all[:, :, first : first + size].reshape(-1))
        first += size
    gain_in, gain_query, gain_key, gain_post_attn, gain_pre, gain_post = full_gains

    inputs = activations[0].astype(f32)
    segment_all = segments[0]
    tok_count = inputs.shape[0]
    first_place = me * tok_count
    place_rows = first_place + jnp.arange(tok_count, dtype=jnp.int32)
    segment_rows = lax.dynamic_slice_in_dim(segment_all, first_place, tok_count)
    earlier = jnp.sum((segment_all[None, :] < segment_rows[:, None]).astype(jnp.int32), axis=1)
    cosine, sine = rope_tables(place_rows - earlier, head_dim)
    length = segment_all.shape[0]
    key_places = (first_place + jnp.arange(length, dtype=jnp.int32)) % length
    key_segments = lax.dynamic_slice_in_dim(
        jnp.concatenate([segment_all, segment_all]), first_place, length
    )
    allowed = (segment_rows[:, None] == key_segments[None, :]) & (
        place_rows[:, None] >= key_places[None, :]
    )
    allowed = jnp.tile(allowed, (heads, 1))

    normed, in_pull = jax.vjp(rms_norm, inputs, gain_in)
    normed_low = normed.astype(bf16)
    qkv = contract(normed_low, full_qkv, 1, 0)
    query_raw = qkv[:, :query_cols].reshape(tok_count, heads, head_dim)
    key_raw = qkv[:, query_cols : query_cols + head_dim]
    value_low = qkv[:, query_cols + head_dim :].astype(bf16)

    def prepare(query_in, key_in, query_scale, key_scale):
        rotated_query = rotate(
            rms_norm(query_in, query_scale), cosine[:, None, :], sine[:, None, :]
        )
        rotated_key = rotate(rms_norm(key_in, key_scale), cosine, sine)
        return (rotated_query, rotated_key)

    (queries, key_rows), prepare_pull = jax.vjp(prepare, query_raw, key_raw, gain_query, gain_key)
    query_low = queries.astype(bf16).transpose(1, 0, 2).reshape(heads * tok_count, head_dim)
    key_value = gather_ahead(jnp.concatenate([key_rows.astype(bf16), value_low], axis=1))
    key_all = key_value[:, :head_dim]
    value_all = key_value[:, head_dim:]

    scores = contract(query_low, key_all, 1, 1) * score_scale
    scores = jnp.where(allowed, scores, far_below)
    top_score = jnp.max(scores, axis=-1, keepdims=True)
    weight = jnp.exp(scores - top_score)
    prob = weight / jnp.sum(weight, axis=-1, keepdims=True)
    prob_low = prob.astype(bf16)
    attended = contract(prob_low, value_all, 1, 0).astype(bf16)
    attended_low = attended.reshape(heads, tok_count, head_dim).transpose(1, 0, 2)
    attended_low = attended_low.reshape(tok_count, query_cols)
    attn_out = contract(attended_low, full_out, 1, 0)
    post_attn, post_attn_pull = jax.vjp(rms_norm, attn_out, gain_post_attn)
    middle = inputs + post_attn
    normed_ff, pre_pull = jax.vjp(rms_norm, middle, gain_pre)
    normed_all = gather_team(normed_ff.astype(bf16))

    gate_up = contract(normed_all, full_both, 1, 0)
    mixed, gated_pull = jax.vjp(gated_unit, gate_up[:, :wide], gate_up[:, wide:])
    mixed_low = mixed.astype(bf16)
    team_half = inner * tok_count
    branch_other = to_ahead(contract(mixed_low[team_half:], full_down, 1, 0, bf16), 1, "core")
    branch_term = contract(mixed_low[:team_half], full_down, 1, 0) + branch_other.astype(f32)
    branch_out = sum_ahead(
        [branch_term[i : i + tok_count] for i in range(0, team_half, tok_count)], "y"
    )
    post_ff, post_pull = jax.vjp(rms_norm, branch_out, gain_post)
    output = (middle + post_ff).astype(bf16)

    grad_output = cotangent[0].astype(f32)
    grad_branch, grad_post_ff = post_pull(grad_output)
    grad_branch_all = gather_team(grad_branch.astype(bf16))
    grad_mixed = contract(grad_branch_all, full_down, 1, 1)
    grad_gate, grad_up = gated_pull(grad_mixed)
    grad_both = jnp.concatenate([grad_gate.astype(bf16), grad_up.astype(bf16)], axis=1)
    grad_normed_term = contract(grad_both, full_both, 1, 1)
    grad_both, mixed_low, grad_normed_term = lax.optimization_barrier(
        (grad_both, mixed_low, grad_normed_term)
    )
    grad_normed_ff = sum_team(grad_normed_term, tok_count)
    down_term = contract(mixed_low, grad_branch_all, 0, 0, bf16)
    both_term = contract(normed_all, grad_both, 0, 0, bf16)
    ffn_terms = jnp.concatenate(
        [
            both_term.reshape(teams, team_rows, 2 * wide),
            jnp.pad(
                down_term.reshape(teams, down_wide, model),
                ((0, 0), (0, team_rows - down_wide), (0, 0)),
            ),
        ],
        axis=2,
    ).reshape(teams * team_rows, -1)
    grad_normed_ff, _ = lax.optimization_barrier((grad_normed_ff, ffn_terms))
    ffn_sum = lax.psum_scatter(ffn_terms.reshape(teams, team_rows, -1), ("x", "z"), scatter_dimension=0, tiled=True)[0]
    down_sum = ffn_sum[:down_wide, 2 * wide :]
    down_two = jnp.concatenate(
        [
            lax.ppermute(down_sum, all_axes, [(b, a) for a, b in before]),
            lax.ppermute(down_sum, all_axes, [(b, a) for a, b in here]),
        ],
        axis=0,
    )
    down_grad = lax.dynamic_slice_in_dim(
        down_two, down_wide - down_shift * (flat % teams), down_rows, 0
    ).astype(f32)

    grad_middle_add, grad_pre_ff = pre_pull(grad_normed_ff)
    grad_middle = grad_output + grad_middle_add
    grad_attn, grad_post_attn = post_attn_pull(grad_middle)
    grad_attn_low = grad_attn.astype(bf16)
    out_term = contract(attended_low, grad_attn_low, 0, 0, bf16)
    grad_attended = contract(grad_attn_low, full_out, 1, 1, bf16)
    grad_attended = grad_attended.reshape(tok_count, heads, head_dim).transpose(1, 0, 2)
    grad_attended = grad_attended.reshape(heads * tok_count, head_dim)

    grad_prob = contract(grad_attended, value_all, 1, 1)
    shift_term = jnp.sum(prob * grad_prob, axis=-1, keepdims=True)
    grad_scores = (prob * (grad_prob - shift_term)).astype(bf16)
    grad_query = contract(grad_scores, key_all, 1, 0) * score_scale
    grad_key = contract(grad_scores, query_low, 0, 0) * score_scale
    grad_value = contract(prob_low, grad_attended, 0, 0)
    grad_key_value = jnp.concatenate([grad_key, grad_value], axis=1)
    grad_key_value = sum_ahead(
        [grad_key_value[s * tok_count : (s + 1) * tok_count] for s in range(inner)]
    )
    grad_queries = grad_query.reshape(heads, tok_count, head_dim).transpose(1, 0, 2)
    grad_query_raw, grad_key_raw, grad_query_gain, grad_key_gain = prepare_pull(
        (grad_queries, grad_key_value[:, :head_dim])
    )
    grad_qkv = jnp.concatenate(
        [
            grad_query_raw.reshape(tok_count, query_cols),
            grad_key_raw,
            grad_key_value[:, head_dim:],
        ],
        axis=1,
    ).astype(bf16)
    qkv_term = contract(normed_low, grad_qkv, 0, 0, bf16)
    grad_normed = contract(grad_qkv, full_qkv, 1, 1)
    grad_input_add, grad_in_gain = in_pull(grad_normed)
    input_grad = grad_middle + grad_input_add

    grad_gains = (
        grad_in_gain,
        grad_query_gain,
        grad_key_gain,
        grad_post_attn,
        grad_pre_ff,
        grad_post_ff,
    )
    gain_terms = jnp.concatenate(
        [item.reshape(teams, members, -1) for item in grad_gains], axis=2
    ).astype(bf16)
    gain_terms = jnp.pad(gain_terms, ((0, 0), (0, 0), (0, model - gain_terms.shape[2])))
    attn_terms = halves(
        qkv_term.reshape(teams, team_rows, qkv_cols),
        jnp.concatenate(
            [out_term.reshape(teams, members * out_rows, model), gain_terms], axis=1
        ),
    )
    attn_half = reduce_axis(attn_terms, "core", 0)
    attn_half = attn_half.reshape(lax.axis_size("x"), lax.axis_size("z"), team_rows, half)
    left = reduce_axis(attn_half[..., :half_qkv], "x", 0)
    right = reduce_axis(attn_half[..., half_qkv:], "z", 1)
    left = reduce_axis(left, "z", 0)
    right = reduce_axis(right, "x", 0)
    attn_sum = jnp.concatenate(
        [
            left.reshape(members, rows, half_qkv),
            jnp.concatenate(
                [
                    right[: members * out_rows].reshape(members, out_rows, half_out),
                    right[members * out_rows :][:, None],
                ],
                axis=1,
            ),
        ],
        axis=2,
    ).reshape(cores, inner, rows, half)
    message = jnp.concatenate(
        [
            ffn_sum[:, : 2 * wide].reshape(cores, inner, rows, 2 * wide),
            attn_sum,
        ],
        axis=3,
    ).transpose(1, 0, 2, 3)
    by_y = swap(message, "y")
    attn_sum = jnp.sum(by_y[..., 2 * wide :].astype(f32), axis=0).astype(bf16)
    message = jnp.concatenate(
        [by_y[c, :, :, : 2 * wide] for c in range(inner)] + [attn_sum], axis=2
    )
    by_core = swap(message, "core").astype(f32)
    both_grad = jnp.concatenate(
        [
            by_core[c, None, :, k * 2 * wide : (k + 1) * 2 * wide]
            for c in range(cores)
            for k in range(inner)
        ],
        axis=0,
    ).transpose(1, 0, 2)
    gate_grad = both_grad[:, :, :part].reshape(rows, members * part)
    up_grad = both_grad[:, :, wide : wide + part].reshape(rows, members * part)
    attn_sum = by_core[:, :, inner * 2 * wide :]
    attn_grad = jnp.concatenate(
        [attn_sum[c, :, :half_qkv] for c in range(cores)]
        + [attn_sum[c, :, half_qkv:] for c in range(cores)],
        axis=1,
    )
    gain_grads = []
    first = qkv_cols
    for item in gains:
        size = item.shape[0]
        gain_grads.append(attn_grad[rows - 1, first : first + size])
        first += size
    return (
        output[None],
        input_grad[None],
        *gain_grads,
        attn_grad[:, :query_cols],
        attn_grad[:, query_cols : query_cols + head_dim],
        attn_grad[:, query_cols + head_dim : qkv_cols],
        attn_grad[:out_rows, qkv_cols : qkv_cols + model],
        gate_grad,
        up_grad,
        down_grad,
    )


def solution(mesh):
    fine = Mesh(mesh.devices.reshape(4, 4, 2, 4), ("x", "z", "core", "y"))
    all_axes = ("x", "z", "core", "y")
    shard = P(all_axes)
    matrix = P(all_axes, None)
    tokens = P(("x", "z", "core"), "y", None)
    return jax.shard_map(
        local,
        mesh=fine,
        in_specs=(tokens, tokens, P(("x", "z", "core"), None)) + (shard,) * 6 + (matrix,) * 7,
        out_specs=(tokens, tokens) + (shard,) * 6 + (matrix,) * 7,
        check_vma=False,
    )
```

profile of v0, /device:TPU:24, one launch (start us, length us, event | category | flops | bytes accessed | tf_op | source)
XLA Modules:
  0.0 406.5 jit_solution(6812657026657095293)
XLA Ops:
  7.2 5.7 %collective-permute-start.8 = (bf16[54,1152]{1,0:T(8,128)(2,1)}, bf16[54,1152]{1,0:T(8,128)(2,1)S(1)}, u32[]{:S(2)}, u32[]{:S(2)}) collective-permute-start(bf16[54,1152]{1,0:T(8,128)(2,1)} %param.31), channel_id=1, source_target_pairs={{0,0},{1,8},{2,16},{3,24},{4,32},{5,40},{6,48},{7,56},{8,64},{9,72... | collective-permute-start | bytes 373256 | tf_op jit(solution)/shard_map/ppermute | solution.py:245
  41.8 5.4 %collective-permute-start.11 = (bf16[72,640]{1,0:T(8,128)(2,1)S(1)}, bf16[72,640]{1,0:T(8,128)(2,1)S(1)}, u32[]{:S(2)}, u32[]{:S(2)}) collective-permute-start(bf16[72,640]{1,0:T(8,128)(2,1)S(1)} %slice.298), channel_id=1, source_target_pairs={{0,16},{8,24},{16,0},{24,8},{1,17},{9,25},{17,1},{25,9},{2,18},{10... | collective-permute-start | bytes 276488 | tf_op jit(solution)/shard_map/ppermute | solution.py:56
  65.1 6.2 %collective-permute-done.13 = bf16[4,72,640]{2,1,0:T(8,128)(2,1)S(1)} collective-permute-done((bf16[4,72,640]{2,1,0:T(8,128)(2,1)S(1)}, bf16[4,72,640]{2,1,0:T(8,128)(2,1)S(1)}, u32[]{:S(2)}, u32[]{:S(2)}) %collective-permute-start.13) | collective-permute-done | bytes 368672 | tf_op jit(solution)/shard_map/ppermute | solution.py:56
  71.3 8.3 %collective-permute-done.14 = bf16[4,72,640]{2,1,0:T(8,128)(2,1)S(1)} collective-permute-done((bf16[4,72,640]{2,1,0:T(8,128)(2,1)S(1)}, bf16[4,72,640]{2,1,0:T(8,128)(2,1)S(1)}, u32[]{:S(2)}, u32[]{:S(2)}) %collective-permute-start.14) | collective-permute-done | bytes 368672 | tf_op jit(solution)/shard_map/ppermute | solution.py:56
  99.4 5.7 %collective-permute-start.26 = (bf16[128,512]{1,0:T(8,128)(2,1)S(1)}, bf16[128,512]{1,0:T(8,128)(2,1)S(1)}, u32[]{:S(2)}, u32[]{:S(2)}) collective-permute-start(bf16[128,512]{1,0:T(8,128)(2,1)S(1)} %pad_maximum_fusion.21), channel_id=1, source_target_pairs={{0,1},{1,2},{2,3},{3,0},{4,5},{5,6},{6,7},{7,4},{8,9},{9,10},{10,1... | collective-permute-start | bytes 393224 | tf_op jit(solution)/shard_map/ppermute | solution.py:51
  107.0 4.2 %collective-permute-done.26 = bf16[128,512]{1,0:T(8,128)(2,1)S(1)} collective-permute-done((bf16[128,512]{1,0:T(8,128)(2,1)S(1)}, bf16[128,512]{1,0:T(8,128)(2,1)S(1)}, u32[]{:S(2)}, u32[]{:S(2)}) %collective-permute-start.26) | collective-permute-done | bytes 131104 | tf_op jit(solution)/shard_map/ppermute | solution.py:51
  123.6 13.1 %collective-permute-done.27 = bf16[128,1152]{1,0:T(8,128)(2,1)S(1)} collective-permute-done((bf16[128,1152]{1,0:T(8,128)(2,1)S(1)}, bf16[128,1152]{1,0:T(8,128)(2,1)S(1)}, u32[]{:S(2)}, u32[]{:S(2)}) %collective-permute-start.27) | collective-permute-done | bytes 294944 | tf_op jit(solution)/shard_map/ppermute | solution.py:51
  137.4 11.9 %collective-permute-start.30 = (bf16[512,1152]{1,0:T(8,128)(2,1)S(1)}, bf16[512,1152]{1,0:T(8,128)(2,1)S(1)}, u32[]{:S(2)}, u32[]{:S(2)}) collective-permute-start(bf16[512,1152]{1,0:T(8,128)(2,1)S(1)} %pad_maximum_fusion.8), channel_id=1, source_target_pairs={{0,4},{4,0},{1,5},{5,1},{2,6},{6,2},{3,7},{7,3},{8,12},{12,8},{9,1... | collective-permute-start | bytes 3538952 | tf_op jit(solution)/shard_map/ppermute | solution.py:51
  155.0 8.5 %fusion.13 = f32[1024,1792]{1,0:T(8,128)S(1)} fusion(bf16[1024,1152]{1,0:T(8,128)(2,1)} %constant_dynamic-update-slice_fusion.6, bf16[1152,2944]{1,0:T(8,128)(2,1)} %all-gather.2.cloned.1.call-done), kind=kOutput, calls=%fused_computation.25 | convolution fusion | flops 4227858432 | bytes 13828096 | tf_op jit(solution)/shard_map/dot_general | solution.py:44
  180.2 5.3 %collective-permute-done.34 = bf16[128,1152]{1,0:T(8,128)(2,1)S(1)} collective-permute-done((bf16[128,1152]{1,0:T(8,128)(2,1)}, bf16[128,1152]{1,0:T(8,128)(2,1)S(1)}, u32[]{:S(2)}, u32[]{:S(2)}) %collective-permute-start.34) | collective-permute-done | bytes 294944 | tf_op jit(solution)/shard_map/ppermute | solution.py:56
  185.4 6.6 %collective-permute-done.33 = bf16[128,1152]{1,0:T(8,128)(2,1)S(1)} collective-permute-done((bf16[128,1152]{1,0:T(8,128)(2,1)S(1)}, bf16[128,1152]{1,0:T(8,128)(2,1)S(1)}, u32[]{:S(2)}, u32[]{:S(2)}) %collective-permute-start.33) | collective-permute-done | bytes 294944 | tf_op jit(solution)/shard_map/ppermute | solution.py:56
  199.8 5.7 %collective-permute-done.35 = bf16[128,1152]{1,0:T(8,128)(2,1)S(1)} collective-permute-done((bf16[128,1152]{1,0:T(8,128)(2,1)S(1)}, bf16[128,1152]{1,0:T(8,128)(2,1)S(1)}, u32[]{:S(2)}, u32[]{:S(2)}) %collective-permute-start.35) | collective-permute-done | bytes 294944 | tf_op jit(solution)/shard_map/ppermute | solution.py:51
  205.6 7.5 %collective-permute-done.36 = bf16[128,1152]{1,0:T(8,128)(2,1)S(1)} collective-permute-done((bf16[128,1152]{1,0:T(8,128)(2,1)S(1)}, bf16[128,1152]{1,0:T(8,128)(2,1)S(1)}, u32[]{:S(2)}, u32[]{:S(2)}) %collective-permute-start.36) | collective-permute-done | bytes 294944 | tf_op jit(solution)/shard_map/ppermute | solution.py:51
  219.9 9.0 %fusion.10 = (bf16[1024,896]{1,0:T(8,128)(2,1)S(1)}, bf16[1024,896]{1,0:T(8,128)(2,1)S(1)}) fusion(f32[1024,1792]{1,0:T(8,128)} %copy-done.2, bf16[1024,1152]{1,0:T(8,128)(2,1)} %constant_dynamic-update-slice_fusion.11, bf16[896,1152]{1,0:T(8,128)(2,1)S(1)} %bitcast.401), kind=kOutput, calls=%fused_computation.19 | convolution fusion | flops 2135949312 | bytes 15433728 | tf_op jit(solution)/shard_map/dot_general | solution.py:44
  229.2 4.9 %fusion.11 = f32[1024,1152]{1,0:T(8,128)S(1)} fusion(bf16[1152,2944]{1,0:T(8,128)(2,1)S(1)} %bitcast.420, bf16[1024,896]{1,0:T(8,128)(2,1)S(1)} %get-tuple-element.47, bf16[1024,896]{1,0:T(8,128)(2,1)S(1)} %get-tuple-element.46), kind=kOutput, calls=%fused_computation.23 | convolution fusion | flops 4235198464 | bytes 12517376 | tf_op jit(solution)/shard_map/dot_general | solution.py:44
  239.1 6.2 %fusion.172 = bf16[1152,1792]{1,0:T(8,128)(2,1)S(1)} fusion(bf16[1024,1152]{1,0:T(8,128)(2,1)} %constant_dynamic-update-slice_fusion.6, bf16[1024,1792]{1,0:T(8,128)(2,1)S(1)} %pad_maximum_fusion), kind=kOutput, calls=%fused_computation.412 | convolution fusion | flops 4227858432 | bytes 10158080 | tf_op jit(solution)/shard_map/dot_general | solution.py:44
  258.0 6.1 %collective-permute-done.41 = bf16[128,1152]{1,0:T(8,128)(2,1)S(1)} collective-permute-done((bf16[128,1152]{1,0:T(8,128)(2,1)S(1)}, bf16[128,1152]{1,0:T(8,128)(2,1)S(1)}, u32[]{:S(2)}, u32[]{:S(2)}) %collective-permute-start.41) | collective-permute-done | bytes 294944 | tf_op jit(solution)/shard_map/ppermute | solution.py:56
  303.3 6.1 %collective-permute-done.46 = bf16[16,72,1408]{2,1,0:T(8,128)(2,1)} collective-permute-done((bf16[16,72,1408]{2,1,0:T(8,128)(2,1)}, bf16[16,72,1408]{2,1,0:T(8,128)(2,1)}, u32[]{:S(2)}, u32[]{:S(2)}) %collective-permute-start.46) | collective-permute-done | bytes 3244064 | tf_op jit(solution)/shard_map/ppermute | solution.py:56
  322.7 4.6 %collective-permute-done.55 = bf16[4,72,640]{2,1,0:T(8,128)(2,1)} collective-permute-done((bf16[4,72,640]{2,1,0:T(8,128)(2,1)}, bf16[4,72,640]{2,1,0:T(8,128)(2,1)}, u32[]{:S(2)}, u32[]{:S(2)}) %collective-permute-start.55) | collective-permute-done | bytes 368672 | tf_op jit(solution)/shard_map/ppermute | solution.py:56
  331.3 11.2 %collective-permute-done.53 = bf16[4,72,640]{2,1,0:T(8,128)(2,1)} collective-permute-done((bf16[4,72,640]{2,1,0:T(8,128)(2,1)}, bf16[4,72,640]{2,1,0:T(8,128)(2,1)}, u32[]{:S(2)}, u32[]{:S(2)}) %collective-permute-start.53) | collective-permute-done | bytes 368672 | tf_op jit(solution)/shard_map/ppermute | solution.py:56
  347.8 4.9 %collective-permute-done.47 = bf16[4,72,768]{2,1,0:T(8,128)(2,1)} collective-permute-done((bf16[4,72,768]{2,1,0:T(8,128)(2,1)}, bf16[4,72,768]{2,1,0:T(8,128)(2,1)}, u32[]{:S(2)}, u32[]{:S(2)}) %collective-permute-start.47) | collective-permute-done | bytes 442400 | tf_op jit(solution)/shard_map/ppermute | solution.py:56
  360.5 4.4 %collective-permute-done.51 = bf16[72,768]{1,0:T(8,128)(2,1)S(1)} collective-permute-done((bf16[72,768]{1,0:T(8,128)(2,1)S(1)}, bf16[72,768]{1,0:T(8,128)(2,1)S(1)}, u32[]{:S(2)}, u32[]{:S(2)}) %collective-permute-start.51) | collective-permute-done | bytes 110624 | tf_op jit(solution)/shard_map/ppermute | solution.py:56
  375.2 6.7 %collective-permute-start.64 = (bf16[56,1152]{1,0:T(8,128)(2,1)S(1)}, bf16[56,1152]{1,0:T(8,128)(2,1)S(1)}, u32[]{:S(2)}, u32[]{:S(2)}) collective-permute-start(bf16[56,1152]{1,0:T(8,128)(2,1)S(1)} %slice.444), channel_id=1, source_target_pairs={{0,0},{8,1},{16,2},{24,3},{32,4},{40,5},{48,6},{56,7},{64,8},{72,9... | collective-permute-start | bytes 387080 | tf_op jit(solution)/shard_map/ppermute | solution.py:375
  382.4 8.7 %collective-permute-done.63 = bf16[56,1152]{1,0:T(8,128)(2,1)S(1)} collective-permute-done((bf16[56,1152]{1,0:T(8,128)(2,1)S(1)}, bf16[56,1152]{1,0:T(8,128)(2,1)S(1)}, u32[]{:S(2)}, u32[]{:S(2)}) %collective-permute-start.63) | collective-permute-done | bytes 129056 | tf_op jit(solution)/shard_map/ppermute | solution.py:374
  (513 shorter events, 222.8 us)
Async XLA Ops:
  7.2 146.0 %all-gather.2.cloned.1.call-start = ((), (), s32[]{:S(2)}) async-start(), calls=%async_computation.1 | async-start | bytes 7206912 | tf_op jit(solution)/shard_map/all_gather | solution.py:252
  7.2 30.6 %collective-permute-start.8 = (bf16[54,1152]{1,0:T(8,128)(2,1)}, bf16[54,1152]{1,0:T(8,128)(2,1)S(1)}, u32[]{:S(2)}, u32[]{:S(2)}) collective-permute-start(bf16[54,1152]{1,0:T(8,128)(2,1)} %param.31), channel_id=1, source_target_pairs={{0,0},{1,8},{2,16},{3,24},{4,32},{5,40},{6,48},{7,56},{8,64},{9,72... | collective-permute-start | bytes 373256 | tf_op jit(solution)/shard_map/ppermute | solution.py:245
  13.0 24.8 %collective-permute-start.9 = (bf16[54,1152]{1,0:T(8,128)(2,1)}, bf16[54,1152]{1,0:T(8,128)(2,1)S(1)}, u32[]{:S(2)}, u32[]{:S(2)}) collective-permute-start(bf16[54,1152]{1,0:T(8,128)(2,1)} %param.31), channel_id=1, source_target_pairs={{1,0},{2,8},{3,16},{4,24},{5,32},{6,40},{7,48},{8,56},{9,64},{10,7... | collective-permute-start | bytes 373256 | tf_op jit(solution)/shard_map/ppermute | solution.py:245
  40.3 326.3 %reduce-scatter.4.cloned.1.call-start = ((), (), s32[]{:S(2)}) async-start(), calls=%async_computation.2 | async-start | bytes 7206912
  53.4 17.8 %collective-permute-start.13 = (bf16[4,72,640]{2,1,0:T(8,128)(2,1)S(1)}, bf16[4,72,640]{2,1,0:T(8,128)(2,1)S(1)}, u32[]{:S(2)}, u32[]{:S(2)}) collective-permute-start(bf16[4,72,640]{2,1,0:T(8,128)(2,1)S(1)} %bitcast_dynamic-update-slice_fusion.12), channel_id=1, source_target_pairs={{0,32},{32,64},{64,96},{96,0},{1,33},{33,65},{65,97},{97,1},{2,34}... | collective-permute-start | bytes 1105928 | tf_op jit(solution)/shard_map/ppermute | solution.py:56
  54.3 25.3 %collective-permute-start.14 = (bf16[4,72,640]{2,1,0:T(8,128)(2,1)S(1)}, bf16[4,72,640]{2,1,0:T(8,128)(2,1)S(1)}, u32[]{:S(2)}, u32[]{:S(2)}) collective-permute-start(bf16[4,72,640]{2,1,0:T(8,128)(2,1)S(1)} %bitcast_dynamic-update-slice_fusion.12), channel_id=1, source_target_pairs={{0,64},{32,96},{64,0},{96,32},{1,65},{33,97},{65,1},{97,33},{2,66}... | collective-permute-start | bytes 1105928 | tf_op jit(solution)/shard_map/ppermute | solution.py:56
  58.5 22.4 %collective-permute-start.15 = (bf16[4,72,640]{2,1,0:T(8,128)(2,1)S(1)}, bf16[4,72,640]{2,1,0:T(8,128)(2,1)S(1)}, u32[]{:S(2)}, u32[]{:S(2)}) collective-permute-start(bf16[4,72,640]{2,1,0:T(8,128)(2,1)S(1)} %bitcast_dynamic-update-slice_fusion.12), channel_id=1, source_target_pairs={{0,96},{32,0},{64,32},{96,64},{1,97},{33,1},{65,33},{97,65},{2,98}... | collective-permute-start | bytes 1105928 | tf_op jit(solution)/shard_map/ppermute | solution.py:56
  62.9 18.2 %collective-permute-start.20 = (bf16[4,72,768]{2,1,0:T(8,128)(2,1)S(1)}, bf16[4,72,768]{2,1,0:T(8,128)(2,1)S(1)}, u32[]{:S(2)}, u32[]{:S(2)}) collective-permute-start(bf16[4,72,768]{2,1,0:T(8,128)(2,1)S(1)} %bitcast_dynamic-update-slice_fusion.8), channel_id=1, source_target_pairs={{0,8},{8,16},{16,24},{24,0},{1,9},{9,17},{17,25},{25,1},{2,10},{10... | collective-permute-start | bytes 1327112 | tf_op jit(solution)/shard_map/ppermute | solution.py:56
  64.7 20.4 %collective-permute-start.21 = (bf16[4,72,768]{2,1,0:T(8,128)(2,1)S(1)}, bf16[4,72,768]{2,1,0:T(8,128)(2,1)S(1)}, u32[]{:S(2)}, u32[]{:S(2)}) collective-permute-start(bf16[4,72,768]{2,1,0:T(8,128)(2,1)S(1)} %bitcast_dynamic-update-slice_fusion.8), channel_id=1, source_target_pairs={{0,16},{8,24},{16,0},{24,8},{1,17},{9,25},{17,1},{25,9},{2,18},{10... | collective-permute-start | bytes 1327112 | tf_op jit(solution)/shard_map/ppermute | solution.py:56
  120.3 16.3 %collective-permute-start.27 = (bf16[128,1152]{1,0:T(8,128)(2,1)S(1)}, bf16[128,1152]{1,0:T(8,128)(2,1)S(1)}, u32[]{:S(2)}, u32[]{:S(2)}) collective-permute-start(bf16[128,1152]{1,0:T(8,128)(2,1)S(1)} %get-tuple-element.43), channel_id=1, source_target_pairs={{0,3},{1,0},{2,1},{3,2},{4,7},{5,4},{6,5},{7,6},{8,11},{9,8},{10,9... | collective-permute-start | bytes 884744 | tf_op jit(solution)/shard_map/ppermute | solution.py:51
  120.3 16.3 %collective-permute-start.28 = (bf16[128,1152]{1,0:T(8,128)(2,1)S(1)}, bf16[128,1152]{1,0:T(8,128)(2,1)S(1)}, u32[]{:S(2)}, u32[]{:S(2)}) collective-permute-start(bf16[128,1152]{1,0:T(8,128)(2,1)S(1)} %get-tuple-element.43), channel_id=1, source_target_pairs={{0,2},{1,3},{2,0},{3,1},{4,6},{5,7},{6,4},{7,5},{8,10},{9,11},{10,... | collective-permute-start | bytes 884744 | tf_op jit(solution)/shard_map/ppermute | solution.py:51
  122.7 14.6 %collective-permute-start.29 = (bf16[128,1152]{1,0:T(8,128)(2,1)S(1)}, bf16[128,1152]{1,0:T(8,128)(2,1)S(1)}, u32[]{:S(2)}, u32[]{:S(2)}) collective-permute-start(bf16[128,1152]{1,0:T(8,128)(2,1)S(1)} %get-tuple-element.43), channel_id=1, source_target_pairs={{0,1},{1,2},{2,3},{3,0},{4,5},{5,6},{6,7},{7,4},{8,9},{9,10},{10,1... | collective-permute-start | bytes 884744 | tf_op jit(solution)/shard_map/ppermute | solution.py:51
  137.4 14.8 %collective-permute-start.30 = (bf16[512,1152]{1,0:T(8,128)(2,1)S(1)}, bf16[512,1152]{1,0:T(8,128)(2,1)S(1)}, u32[]{:S(2)}, u32[]{:S(2)}) collective-permute-start(bf16[512,1152]{1,0:T(8,128)(2,1)S(1)} %pad_maximum_fusion.8), channel_id=1, source_target_pairs={{0,4},{4,0},{1,5},{5,1},{2,6},{6,2},{3,7},{7,3},{8,12},{12,8},{9,1... | collective-permute-start | bytes 3538952 | tf_op jit(solution)/shard_map/ppermute | solution.py:51
  174.9 17.1 %collective-permute-start.33 = (bf16[128,1152]{1,0:T(8,128)(2,1)S(1)}, bf16[128,1152]{1,0:T(8,128)(2,1)S(1)}, u32[]{:S(2)}, u32[]{:S(2)}) collective-permute-start(bf16[128,1152]{1,0:T(8,128)(2,1)S(1)} %get-tuple-element.71), channel_id=1, source_target_pairs={{0,2},{1,3},{2,0},{3,1},{4,6},{5,7},{6,4},{7,5},{8,10},{9,11},{10,... | collective-permute-start | bytes 884744 | tf_op jit(solution)/shard_map/ppermute | solution.py:56
  196.0 17.1 %collective-permute-start.36 = (bf16[128,1152]{1,0:T(8,128)(2,1)S(1)}, bf16[128,1152]{1,0:T(8,128)(2,1)S(1)}, u32[]{:S(2)}, u32[]{:S(2)}) collective-permute-start(bf16[128,1152]{1,0:T(8,128)(2,1)S(1)} %get-tuple-element.39), channel_id=1, source_target_pairs={{0,2},{1,3},{2,0},{3,1},{4,6},{5,7},{6,4},{7,5},{8,10},{9,11},{10,... | collective-permute-start | bytes 884744 | tf_op jit(solution)/shard_map/ppermute | solution.py:51
  247.2 16.8 %collective-permute-start.41 = (bf16[128,1152]{1,0:T(8,128)(2,1)S(1)}, bf16[128,1152]{1,0:T(8,128)(2,1)S(1)}, u32[]{:S(2)}, u32[]{:S(2)}) collective-permute-start(bf16[128,1152]{1,0:T(8,128)(2,1)S(1)} %get-tuple-element.68), channel_id=1, source_target_pairs={{0,2},{1,3},{2,0},{3,1},{4,6},{5,7},{6,4},{7,5},{8,10},{9,11},{10,... | collective-permute-start | bytes 884744 | tf_op jit(solution)/shard_map/ppermute | solution.py:56
  316.2 15.1 %collective-permute-start.54 = (bf16[4,72,640]{2,1,0:T(8,128)(2,1)}, bf16[4,72,640]{2,1,0:T(8,128)(2,1)}, u32[]{:S(2)}, u32[]{:S(2)}) collective-permute-start(bf16[4,72,640]{2,1,0:T(8,128)(2,1)} %get-tuple-element.60), channel_id=1, source_target_pairs={{0,16},{8,24},{16,0},{24,8},{1,17},{9,25},{17,1},{25,9},{2,18},{10... | collective-permute-start | bytes 1105928 | tf_op jit(solution)/shard_map/ppermute | solution.py:56
  316.7 25.8 %collective-permute-start.53 = (bf16[4,72,640]{2,1,0:T(8,128)(2,1)}, bf16[4,72,640]{2,1,0:T(8,128)(2,1)}, u32[]{:S(2)}, u32[]{:S(2)}) collective-permute-start(bf16[4,72,640]{2,1,0:T(8,128)(2,1)} %get-tuple-element.59), channel_id=1, source_target_pairs={{0,8},{8,16},{16,24},{24,0},{1,9},{9,17},{17,25},{25,1},{2,10},{10... | collective-permute-start | bytes 1105928 | tf_op jit(solution)/shard_map/ppermute | solution.py:56
  319.8 27.1 %collective-permute-start.49 = (bf16[4,72,768]{2,1,0:T(8,128)(2,1)}, bf16[4,72,768]{2,1,0:T(8,128)(2,1)}, u32[]{:S(2)}, u32[]{:S(2)}) collective-permute-start(bf16[4,72,768]{2,1,0:T(8,128)(2,1)} %get-tuple-element.57), channel_id=1, source_target_pairs={{0,96},{32,0},{64,32},{96,64},{1,97},{33,1},{65,33},{97,65},{2,98}... | collective-permute-start | bytes 1327112 | tf_op jit(solution)/shard_map/ppermute | solution.py:56
  322.7 25.2 %collective-permute-start.48 = (bf16[4,72,768]{2,1,0:T(8,128)(2,1)}, bf16[4,72,768]{2,1,0:T(8,128)(2,1)}, u32[]{:S(2)}, u32[]{:S(2)}) collective-permute-start(bf16[4,72,768]{2,1,0:T(8,128)(2,1)} %get-tuple-element.58), channel_id=1, source_target_pairs={{0,64},{32,96},{64,0},{96,32},{1,65},{33,97},{65,1},{97,33},{2,66}... | collective-permute-start | bytes 1327112 | tf_op jit(solution)/shard_map/ppermute | solution.py:56
  327.3 25.5 %collective-permute-start.47 = (bf16[4,72,768]{2,1,0:T(8,128)(2,1)}, bf16[4,72,768]{2,1,0:T(8,128)(2,1)}, u32[]{:S(2)}, u32[]{:S(2)}) collective-permute-start(bf16[4,72,768]{2,1,0:T(8,128)(2,1)} %get-tuple-element.56), channel_id=1, source_target_pairs={{0,32},{32,64},{64,96},{96,0},{1,33},{33,65},{65,97},{97,1},{2,34}... | collective-permute-start | bytes 1327112 | tf_op jit(solution)/shard_map/ppermute | solution.py:56
  344.0 14.6 %collective-permute-start.58 = (bf16[72,640]{1,0:T(8,128)(2,1)S(1)}, bf16[72,640]{1,0:T(8,128)(2,1)S(1)}, u32[]{:S(2)}, u32[]{:S(2)}) collective-permute-start(bf16[72,640]{1,0:T(8,128)(2,1)S(1)} %get-tuple-element.101), channel_id=1, source_target_pairs={{0,96},{32,0},{64,32},{96,64},{1,97},{33,1},{65,33},{97,65},{2,98}... | collective-permute-start | bytes 276488 | tf_op jit(solution)/shard_map/ppermute | solution.py:56
  372.7 18.4 %collective-permute-start.63 = (bf16[56,1152]{1,0:T(8,128)(2,1)S(1)}, bf16[56,1152]{1,0:T(8,128)(2,1)S(1)}, u32[]{:S(2)}, u32[]{:S(2)}) collective-permute-start(bf16[56,1152]{1,0:T(8,128)(2,1)S(1)} %slice.444), channel_id=1, source_target_pairs={{0,1},{8,2},{16,3},{24,4},{32,5},{40,6},{48,7},{56,8},{64,9},{72,1... | collective-permute-start | bytes 387080 | tf_op jit(solution)/shard_map/ppermute | solution.py:374
  375.2 18.0 %collective-permute-start.64 = (bf16[56,1152]{1,0:T(8,128)(2,1)S(1)}, bf16[56,1152]{1,0:T(8,128)(2,1)S(1)}, u32[]{:S(2)}, u32[]{:S(2)}) collective-permute-start(bf16[56,1152]{1,0:T(8,128)(2,1)S(1)} %slice.444), channel_id=1, source_target_pairs={{0,0},{8,1},{16,2},{24,3},{32,4},{40,5},{48,6},{56,7},{64,8},{72,9... | collective-permute-start | bytes 387080 | tf_op jit(solution)/shard_map/ppermute | solution.py:375
  (121 other events, 971.5 us)
Sparse Core Ops, SparseCore 0:
  40.4 82.1 all-gather.1
  254.1 99.6 reduce-scatter.3
where the time goes:
time: 411 us; the launch traced here: 406 us
  waiting for transfers between devices  135 us (33%)
  starting transfers between devices  108 us (26%)
  local copies, waits for them, and re-layouts  51 us (12%)
  matrix products  48.8 us (12%)
  other arithmetic  47.5 us (12%)
  between operations  16.7 us (4%)
    ppermute x50, waiting for transfers between devices, to_ahead(): lax.ppermute(block, axis, [(i, (i + step) % size) for i in range(size)])  88.6 us
    ppermute x50, starting transfers between devices, to_ahead(): lax.ppermute(block, axis, [(i, (i + step) % size) for i in range(size)])  64.4 us
    dot_general x19, matrix products, contract(): lax.dot_general(left, right, (((left_dim,), (right_dim,)), ((), ())), pre...  48.8 us
    ppermute x11, waiting for transfers between devices, from_ahead(): lax.ppermute(block, axis, [(i, (i - step) % size) for i in range(size)])  35.3 us
    ppermute x11, starting transfers between devices, from_ahead(): lax.ppermute(block, axis, [(i, (i - step) % size) for i in range(size)])  25.8 us
    unnamed x173, local copies, waits for them, and re-layouts  12.6 us
    ppermute x1, waiting for transfers between devices, local(): lax.ppermute(down_sum, all_axes, [(b, a) for a, b in before])  8.7 us
  transfers between devices with their start and end apart: 67, of which 35 were waited for; matrix products, arithmetic and copies ran while one was open for 23% of the time, Pallas kernels for 0%

commit v1 on v0

--- a/solution.py
+++ b/solution.py
@@ -217,6 +217,7 @@
         jnp.concatenate([w_out, gain_row], axis=0),
     )
     attn_rows = gather_blocks(attn_rows, "y").transpose(1, 0, 2, 3)
+    attn_rows, w_down = lax.optimization_barrier((attn_rows, w_down))
     attn_rows = swap(attn_rows, "core").reshape(members, rows, half)
     attn_shard = jnp.concatenate(
         [
@@ -250,12 +251,14 @@
         axis=1,
     )
     full = lax.all_gather(shard, ("x", "z"), axis=0, tiled=True)
-    attn_shard, _ = lax.optimization_barrier((attn_shard, shard))
     full_both = full[:, : 2 * wide]
     full_down = full.reshape(teams, team_rows, -1)[:, :down_wide, 2 * wide :].reshape(wide, model)
 
-    left = gather_axis(gather_axis(attn_shard[:, :half_qkv], "x", 0), "z", 1)
-    right = gather_axis(gather_axis(attn_shard[:, half_qkv:], "z", 0), "x", 0)
+    left = gather_axis(attn_shard[:, :half_qkv], "x", 0)
+    right = gather_axis(attn_shard[:, half_qkv:], "z", 0)
+    left, right, _ = lax.optimization_barrier((left, right, shard))
+    left = gather_axis(left, "z", 1)
+    right = gather_axis(right, "x", 0)
     left = by_sender([left, to_ahead(left, 1, "core")], "core")
     right = by_sender([right, to_ahead(right, 1, "core")], "core")
     right = right.reshape(cores, teams, team_rows, half_out)
@@ -368,17 +371,6 @@
     ).reshape(teams * team_rows, -1)
     grad_normed_ff, _ = lax.optimization_barrier((grad_normed_ff, ffn_terms))
     ffn_sum = lax.psum_scatter(ffn_terms.reshape(teams, team_rows, -1), ("x", "z"), scatter_dimension=0, tiled=True)[0]
-    down_sum = ffn_sum[:down_wide, 2 * wide :]
-    down_two = jnp.concatenate(
-        [
-            lax.ppermute(down_sum, all_axes, [(b, a) for a, b in before]),
-            lax.ppermute(down_sum, all_axes, [(b, a) for a, b in here]),
-        ],
-        axis=0,
-    )
-    down_grad = lax.dynamic_slice_in_dim(
-        down_two, down_wide - down_shift * (flat % teams), down_rows, 0
-    ).astype(f32)
 
     grad_middle_add, grad_pre_ff = pre_pull(grad_normed_ff)
     grad_middle = grad_output + grad_middle_add
@@ -438,6 +430,7 @@
     attn_half = attn_half.reshape(lax.axis_size("x"), lax.axis_size("z"), team_rows, half)
     left = reduce_axis(attn_half[..., :half_qkv], "x", 0)
     right = reduce_axis(attn_half[..., half_qkv:], "z", 1)
+    right, ffn_sum = lax.optimization_barrier((right, ffn_sum))
     left = reduce_axis(left, "z", 0)
     right = reduce_axis(right, "x", 0)
     attn_sum = jnp.concatenate(
@@ -453,6 +446,19 @@
         ],
         axis=2,
     ).reshape(cores, inner, rows, half)
+    down_sum = ffn_sum[:down_wide, 2 * wide :]
+    down_two = jnp.concatenate(
+        [
+            lax.ppermute(down_sum, all_axes, [(b, a) for a, b in before]),
+            lax.ppermute(down_sum, all_axes, [(b, a) for a, b in here]),
+        ],
+        axis=0,
+    )
+    down_grad = lax.dynamic_slice_in_dim(
+        down_two, down_wide - down_shift * (flat % teams), down_rows, 0
+    ).astype(f32)
+    attn_sum, down_grad = lax.optimization_barrier((attn_sum, down_grad))
+
     message = jnp.concatenate(
         [
             ffn_sum[:, : 2 * wide].reshape(cores, inner, rows, 2 * wide),

time: 411 us -> 422 us (1.027)
  the two profiles are of different devices: /device:TPU:24 before, /device:TPU:1 now
where the time goes in v1:
time: 422 us; the launch traced here: 419 us
  waiting for transfers between devices  136 us (32%)
  starting transfers between devices  121 us (29%)
  local copies, waits for them, and re-layouts  49.7 us (12%)
  matrix products  49 us (12%)
  other arithmetic  46.1 us (11%)
  between operations  16.7 us (4%)
    ppermute x50, waiting for transfers between devices, to_ahead(): lax.ppermute(block, axis, [(i, (i + step) % size) for i in range(size)])  99.8 us
    ppermute x50, starting transfers between devices, to_ahead(): lax.ppermute(block, axis, [(i, (i + step) % size) for i in range(size)])  79.6 us
    dot_general x19, matrix products, contract(): lax.dot_general(left, right, (((left_dim,), (right_dim,)), ((), ())), pre...  49 us
    ppermute x11, waiting for transfers between devices, from_ahead(): lax.ppermute(block, axis, [(i, (i - step) % size) for i in range(size)])  35.6 us
    ppermute x11, starting transfers between devices, from_ahead(): lax.ppermute(block, axis, [(i, (i - step) % size) for i in range(size)])  22.7 us
    unnamed x176, local copies, waits for them, and re-layouts  12.6 us
  transfers between devices with their start and end apart: 67, of which 41 were waited for; matrix products, arithmetic and copies ran while one was open for 20% of the time, Pallas kernels for 0%

profile of v1, /device:TPU:1, one launch (start us, length us, event | category | flops | bytes accessed | tf_op | source)
XLA Modules:
  0.0 418.6 jit_solution(8239416541952994825)
XLA Ops:
  22.7 5.1 %collective-permute-start.14 = (bf16[54,1152]{1,0:T(8,128)(2,1)S(1)}, bf16[54,1152]{1,0:T(8,128)(2,1)S(1)}, u32[]{:S(2)}, u32[]{:S(2)}) collective-permute-start(bf16[54,1152]{1,0:T(8,128)(2,1)S(1)} %copy-done.74), channel_id=1, source_target_pairs={{0,0},{1,8},{2,16},{3,24},{4,32},{5,40},{6,48},{7,56},{8,64},{9,72... | collective-permute-start | bytes 373256 | tf_op jit(solution)/shard_map/ppermute | solution.py:246
  27.8 7.3 %collective-permute-start.15 = (bf16[54,1152]{1,0:T(8,128)(2,1)S(1)}, bf16[54,1152]{1,0:T(8,128)(2,1)S(1)}, u32[]{:S(2)}, u32[]{:S(2)}) collective-permute-start(bf16[54,1152]{1,0:T(8,128)(2,1)S(1)} %copy-done.74), channel_id=1, source_target_pairs={{1,0},{2,8},{3,16},{4,24},{5,32},{6,40},{7,48},{8,56},{9,64},{10,7... | collective-permute-start | bytes 373256 | tf_op jit(solution)/shard_map/ppermute | solution.py:246
  61.5 4.6 %collective-permute-start.21 = (bf16[4,72,768]{2,1,0:T(8,128)(2,1)S(1)}, bf16[4,72,768]{2,1,0:T(8,128)(2,1)S(1)}, u32[]{:S(2)}, u32[]{:S(2)}) collective-permute-start(bf16[4,72,768]{2,1,0:T(8,128)(2,1)S(1)} %bitcast_dynamic-update-slice_fusion.8), channel_id=1, source_target_pairs={{0,16},{8,24},{16,0},{24,8},{1,17},{9,25},{17,1},{25,9},{2,18},{10... | collective-permute-start | bytes 1327112 | tf_op jit(solution)/shard_map/ppermute | solution.py:56
  66.5 7.5 %collective-permute-done.16 = bf16[4,72,640]{2,1,0:T(8,128)(2,1)S(1)} collective-permute-done((bf16[4,72,640]{2,1,0:T(8,128)(2,1)S(1)}, bf16[4,72,640]{2,1,0:T(8,128)(2,1)S(1)}, u32[]{:S(2)}, u32[]{:S(2)}) %collective-permute-start.16) | collective-permute-done | bytes 368672 | tf_op jit(solution)/shard_map/ppermute | solution.py:56
  80.6 5.0 %collective-permute-start.19 = (bf16[4,4,72,640]{3,2,1,0:T(8,128)(2,1)S(1)}, bf16[4,4,72,640]{3,2,1,0:T(8,128)(2,1)}, u32[]{:S(2)}, u32[]{:S(2)}) collective-permute-start(bf16[4,4,72,640]{3,2,1,0:T(8,128)(2,1)S(1)} %bitcast_dynamic-update-slice_fusion.4), channel_id=1, source_target_pairs={{0,4},{4,0},{1,5},{5,1},{2,6},{6,2},{3,7},{7,3},{8,12},{12,8},{9,1... | collective-permute-start | bytes 4423688 | tf_op jit(solution)/shard_map/ppermute | solution.py:56
  85.8 14.9 %collective-permute-start.23 = (bf16[4,4,72,768]{3,2,1,0:T(8,128)(2,1)S(1)}, bf16[4,4,72,768]{3,2,1,0:T(8,128)(2,1)}, u32[]{:S(2)}, u32[]{:S(2)}) collective-permute-start(bf16[4,4,72,768]{3,2,1,0:T(8,128)(2,1)S(1)} %bitcast_dynamic-update-slice_fusion.3), channel_id=1, source_target_pairs={{0,4},{4,0},{1,5},{5,1},{2,6},{6,2},{3,7},{7,3},{8,12},{12,8},{9,1... | collective-permute-start | bytes 5308424 | tf_op jit(solution)/shard_map/ppermute | solution.py:56
  133.8 5.9 %collective-permute-done.27 = bf16[128,1152]{1,0:T(8,128)(2,1)S(1)} collective-permute-done((bf16[128,1152]{1,0:T(8,128)(2,1)S(1)}, bf16[128,1152]{1,0:T(8,128)(2,1)S(1)}, u32[]{:S(2)}, u32[]{:S(2)}) %collective-permute-start.27) | collective-permute-done | bytes 294944 | tf_op jit(solution)/shard_map/ppermute | solution.py:51
  142.2 7.5 %collective-permute-done.29 = bf16[128,1152]{1,0:T(8,128)(2,1)S(1)} collective-permute-done((bf16[128,1152]{1,0:T(8,128)(2,1)S(1)}, bf16[128,1152]{1,0:T(8,128)(2,1)S(1)}, u32[]{:S(2)}, u32[]{:S(2)}) %collective-permute-start.29) | collective-permute-done | bytes 294944 | tf_op jit(solution)/shard_map/ppermute | solution.py:51
  149.8 12.4 %collective-permute-start.30 = (bf16[512,1152]{1,0:T(8,128)(2,1)S(1)}, bf16[512,1152]{1,0:T(8,128)(2,1)S(1)}, u32[]{:S(2)}, u32[]{:S(2)}) collective-permute-start(bf16[512,1152]{1,0:T(8,128)(2,1)S(1)} %pad_maximum_fusion.8), channel_id=1, source_target_pairs={{0,4},{4,0},{1,5},{5,1},{2,6},{6,2},{3,7},{7,3},{8,12},{12,8},{9,1... | collective-permute-start | bytes 3538952 | tf_op jit(solution)/shard_map/ppermute | solution.py:51
  167.6 8.5 %fusion.13 = f32[1024,1792]{1,0:T(8,128)S(1)} fusion(bf16[1024,1152]{1,0:T(8,128)(2,1)} %constant_dynamic-update-slice_fusion.6, bf16[1152,2944]{1,0:T(8,128)(2,1)} %all-gather.2.cloned.1.call-done), kind=kOutput, calls=%fused_computation.25 | convolution fusion | flops 4227858432 | bytes 13828096 | tf_op jit(solution)/shard_map/dot_general | solution.py:44
  190.6 5.1 %collective-permute-done.34 = bf16[128,1152]{1,0:T(8,128)(2,1)S(1)} collective-permute-done((bf16[128,1152]{1,0:T(8,128)(2,1)}, bf16[128,1152]{1,0:T(8,128)(2,1)S(1)}, u32[]{:S(2)}, u32[]{:S(2)}) %collective-permute-start.34) | collective-permute-done | bytes 294944 | tf_op jit(solution)/shard_map/ppermute | solution.py:56
  197.0 7.3 %collective-permute-done.32 = bf16[128,1152]{1,0:T(8,128)(2,1)S(1)} collective-permute-done((bf16[128,1152]{1,0:T(8,128)(2,1)S(1)}, bf16[128,1152]{1,0:T(8,128)(2,1)S(1)}, u32[]{:S(2)}, u32[]{:S(2)}) %collective-permute-start.32) | collective-permute-done | bytes 294944 | tf_op jit(solution)/shard_map/ppermute | solution.py:56
  209.9 6.4 %collective-permute-done.35 = bf16[128,1152]{1,0:T(8,128)(2,1)S(1)} collective-permute-done((bf16[128,1152]{1,0:T(8,128)(2,1)S(1)}, bf16[128,1152]{1,0:T(8,128)(2,1)S(1)}, u32[]{:S(2)}, u32[]{:S(2)}) %collective-permute-start.35) | collective-permute-done | bytes 294944 | tf_op jit(solution)/shard_map/ppermute | solution.py:51
  216.8 8.2 %collective-permute-done.37 = bf16[128,1152]{1,0:T(8,128)(2,1)S(1)} collective-permute-done((bf16[128,1152]{1,0:T(8,128)(2,1)S(1)}, bf16[128,1152]{1,0:T(8,128)(2,1)S(1)}, u32[]{:S(2)}, u32[]{:S(2)}) %collective-permute-start.37) | collective-permute-done | bytes 294944 | tf_op jit(solution)/shard_map/ppermute | solution.py:51
  232.3 9.0 %fusion.10 = (bf16[1024,896]{1,0:T(8,128)(2,1)S(1)}, bf16[1024,896]{1,0:T(8,128)(2,1)S(1)}) fusion(f32[1024,1792]{1,0:T(8,128)} %copy-done.2, bf16[1024,1152]{1,0:T(8,128)(2,1)} %constant_dynamic-update-slice_fusion.11, bf16[896,1152]{1,0:T(8,128)(2,1)S(1)} %bitcast.401), kind=kOutput, calls=%fused_computation.19 | convolution fusion | flops 2135949312 | bytes 15433728 | tf_op jit(solution)/shard_map/dot_general | solution.py:44
  241.5 4.9 %fusion.11 = f32[1024,1152]{1,0:T(8,128)S(1)} fusion(bf16[1152,2944]{1,0:T(8,128)(2,1)S(1)} %bitcast.422, bf16[1024,896]{1,0:T(8,128)(2,1)S(1)} %get-tuple-element.61, bf16[1024,896]{1,0:T(8,128)(2,1)S(1)} %get-tuple-element.60), kind=kOutput, calls=%fused_computation.23 | convolution fusion | flops 4235198464 | bytes 12517376 | tf_op jit(solution)/shard_map/dot_general | solution.py:44
  251.1 6.2 %fusion.172 = bf16[1152,1792]{1,0:T(8,128)(2,1)S(1)} fusion(bf16[1024,1152]{1,0:T(8,128)(2,1)} %constant_dynamic-update-slice_fusion.6, bf16[1024,1792]{1,0:T(8,128)(2,1)S(1)} %pad_maximum_fusion), kind=kOutput, calls=%fused_computation.414 | convolution fusion | flops 4227858432 | bytes 10158080 | tf_op jit(solution)/shard_map/dot_general | solution.py:44
  269.5 7.4 %collective-permute-done.40 = bf16[128,1152]{1,0:T(8,128)(2,1)} collective-permute-done((bf16[128,1152]{1,0:T(8,128)(2,1)S(1)}, bf16[128,1152]{1,0:T(8,128)(2,1)}, u32[]{:S(2)}, u32[]{:S(2)}) %collective-permute-start.40) | collective-permute-done | bytes 294944 | tf_op jit(solution)/shard_map/ppermute | solution.py:56
  315.7 5.8 %collective-permute-done.46 = bf16[16,72,1408]{2,1,0:T(8,128)(2,1)} collective-permute-done((bf16[16,72,1408]{2,1,0:T(8,128)(2,1)}, bf16[16,72,1408]{2,1,0:T(8,128)(2,1)}, u32[]{:S(2)}, u32[]{:S(2)}) %collective-permute-start.46) | collective-permute-done | bytes 3244064 | tf_op jit(solution)/shard_map/ppermute | solution.py:56
  343.3 13.4 %collective-permute-done.50 = bf16[4,72,768]{2,1,0:T(8,128)(2,1)S(1)} collective-permute-done((bf16[4,72,768]{2,1,0:T(8,128)(2,1)S(1)}, bf16[4,72,768]{2,1,0:T(8,128)(2,1)S(1)}, u32[]{:S(2)}, u32[]{:S(2)}) %collective-permute-start.50) | collective-permute-done | bytes 442400 | tf_op jit(solution)/shard_map/ppermute | solution.py:56
  369.0 4.7 %collective-permute-start.59 = (bf16[56,1152]{1,0:T(8,128)(2,1)S(1)}, bf16[56,1152]{1,0:T(8,128)(2,1)S(1)}, u32[]{:S(2)}, u32[]{:S(2)}) collective-permute-start(bf16[56,1152]{1,0:T(8,128)(2,1)S(1)} %slice.341), channel_id=1, source_target_pairs={{0,1},{8,2},{16,3},{24,4},{32,5},{40,6},{48,7},{56,8},{64,9},{72,1... | collective-permute-start | bytes 387080 | tf_op jit(solution)/shard_map/ppermute | solution.py:452
  385.9 5.5 %collective-permute-start.61 = (bf16[2,9,3200]{2,1,0:T(8,128)(2,1)S(1)}, bf16[2,9,3200]{2,1,0:T(8,128)(2,1)S(1)}, u32[]{:S(2)}, u32[]{:S(2)}) collective-permute-start(bf16[2,9,3200]{2,1,0:T(8,128)(2,1)S(1)} %get-tuple-element.92), channel_id=1, source_target_pairs={{0,3},{1,0},{2,1},{3,2},{4,7},{5,4},{6,5},{7,6},{8,11},{9,8},{10,9... | collective-permute-start | bytes 345608 | tf_op jit(solution)/shard_map/ppermute | solution.py:56
  392.1 4.8 %collective-permute-done.61 = bf16[2,9,3200]{2,1,0:T(8,128)(2,1)S(1)} collective-permute-done((bf16[2,9,3200]{2,1,0:T(8,128)(2,1)S(1)}, bf16[2,9,3200]{2,1,0:T(8,128)(2,1)S(1)}, u32[]{:S(2)}, u32[]{:S(2)}) %collective-permute-start.61) | collective-permute-done | bytes 115232 | tf_op jit(solution)/shard_map/ppermute | solution.py:56
  397.7 4.9 %collective-permute-done.63 = bf16[2,9,3200]{2,1,0:T(8,128)(2,1)S(1)} collective-permute-done((bf16[2,9,3200]{2,1,0:T(8,128)(2,1)S(1)}, bf16[2,9,3200]{2,1,0:T(8,128)(2,1)S(1)}, u32[]{:S(2)}, u32[]{:S(2)}) %collective-permute-start.63) | collective-permute-done | bytes 115232 | tf_op jit(solution)/shard_map/ppermute | solution.py:56
  (516 shorter events, 229.6 us)
Async XLA Ops:
  7.2 158.6 %all-gather.2.cloned.1.call-start = ((), (), s32[]{:S(2)}) async-start(), calls=%async_computation.1 | async-start | bytes 7206912 | tf_op jit(solution)/shard_map/all_gather | solution.py:253
  18.1 17.1 %collective-permute-start.10 = (bf16[9,3584]{1,0:T(8,128)(2,1)S(1)}, bf16[9,3584]{1,0:T(8,128)(2,1)S(1)}, u32[]{:S(2)}, u32[]{:S(2)}) collective-permute-start(bf16[9,3584]{1,0:T(8,128)(2,1)S(1)} %bitcast.434), channel_id=1, source_target_pairs={{0,3},{1,0},{2,1},{3,2},{4,7},{5,4},{6,5},{7,6},{8,11},{9,8},{10,9... | collective-permute-start | bytes 193544 | tf_op jit(solution)/shard_map/ppermute | solution.py:56
  20.2 15.1 %collective-permute-start.11 = (bf16[9,3584]{1,0:T(8,128)(2,1)S(1)}, bf16[9,3584]{1,0:T(8,128)(2,1)S(1)}, u32[]{:S(2)}, u32[]{:S(2)}) collective-permute-start(bf16[9,3584]{1,0:T(8,128)(2,1)S(1)} %bitcast.433), channel_id=1, source_target_pairs={{0,2},{1,3},{2,0},{3,1},{4,6},{5,7},{6,4},{7,5},{8,10},{9,11},{10,... | collective-permute-start | bytes 193544 | tf_op jit(solution)/shard_map/ppermute | solution.py:56
  22.7 14.6 %collective-permute-start.14 = (bf16[54,1152]{1,0:T(8,128)(2,1)S(1)}, bf16[54,1152]{1,0:T(8,128)(2,1)S(1)}, u32[]{:S(2)}, u32[]{:S(2)}) collective-permute-start(bf16[54,1152]{1,0:T(8,128)(2,1)S(1)} %copy-done.74), channel_id=1, source_target_pairs={{0,0},{1,8},{2,16},{3,24},{4,32},{5,40},{6,48},{7,56},{8,64},{9,72... | collective-permute-start | bytes 373256 | tf_op jit(solution)/shard_map/ppermute | solution.py:246
  39.6 327.6 %reduce-scatter.4.cloned.1.call-start = ((), (), s32[]{:S(2)}) async-start(), calls=%async_computation.2 | async-start | bytes 7206912
  40.1 18.3 %collective-permute-start.4 = (bf16[72,768]{1,0:T(8,128)(2,1)S(1)}, bf16[72,768]{1,0:T(8,128)(2,1)S(1)}, u32[]{:S(2)}, u32[]{:S(2)}) collective-permute-start(bf16[72,768]{1,0:T(8,128)(2,1)S(1)} %reshape.493), channel_id=1, source_target_pairs={{0,32},{32,64},{64,96},{96,0},{1,33},{33,65},{65,97},{97,1},{2,34}... | collective-permute-start | bytes 331784 | tf_op jit(solution)/shard_map/ppermute | solution.py:56
  58.4 15.5 %collective-permute-start.16 = (bf16[4,72,640]{2,1,0:T(8,128)(2,1)S(1)}, bf16[4,72,640]{2,1,0:T(8,128)(2,1)S(1)}, u32[]{:S(2)}, u32[]{:S(2)}) collective-permute-start(bf16[4,72,640]{2,1,0:T(8,128)(2,1)S(1)} %bitcast_dynamic-update-slice_fusion.11), channel_id=1, source_target_pairs={{0,32},{32,64},{64,96},{96,0},{1,33},{33,65},{65,97},{97,1},{2,34}... | collective-permute-start | bytes 1105928 | tf_op jit(solution)/shard_map/ppermute | solution.py:56
  58.5 20.5 %collective-permute-start.17 = (bf16[4,72,640]{2,1,0:T(8,128)(2,1)S(1)}, bf16[4,72,640]{2,1,0:T(8,128)(2,1)S(1)}, u32[]{:S(2)}, u32[]{:S(2)}) collective-permute-start(bf16[4,72,640]{2,1,0:T(8,128)(2,1)S(1)} %bitcast_dynamic-update-slice_fusion.11), channel_id=1, source_target_pairs={{0,64},{32,96},{64,0},{96,32},{1,65},{33,97},{65,1},{97,33},{2,66}... | collective-permute-start | bytes 1105928 | tf_op jit(solution)/shard_map/ppermute | solution.py:56
  59.5 21.1 %collective-permute-start.18 = (bf16[4,72,640]{2,1,0:T(8,128)(2,1)S(1)}, bf16[4,72,640]{2,1,0:T(8,128)(2,1)S(1)}, u32[]{:S(2)}, u32[]{:S(2)}) collective-permute-start(bf16[4,72,640]{2,1,0:T(8,128)(2,1)S(1)} %bitcast_dynamic-update-slice_fusion.11), channel_id=1, source_target_pairs={{0,96},{32,0},{64,32},{96,64},{1,97},{33,1},{65,33},{97,65},{2,98}... | collective-permute-start | bytes 1105928 | tf_op jit(solution)/shard_map/ppermute | solution.py:56
  61.2 24.5 %collective-permute-start.20 = (bf16[4,72,768]{2,1,0:T(8,128)(2,1)S(1)}, bf16[4,72,768]{2,1,0:T(8,128)(2,1)S(1)}, u32[]{:S(2)}, u32[]{:S(2)}) collective-permute-start(bf16[4,72,768]{2,1,0:T(8,128)(2,1)S(1)} %bitcast_dynamic-update-slice_fusion.8), channel_id=1, source_target_pairs={{0,8},{8,16},{16,24},{24,0},{1,9},{9,17},{17,25},{25,1},{2,10},{10... | collective-permute-start | bytes 1327112 | tf_op jit(solution)/shard_map/ppermute | solution.py:56
  61.5 24.2 %collective-permute-start.21 = (bf16[4,72,768]{2,1,0:T(8,128)(2,1)S(1)}, bf16[4,72,768]{2,1,0:T(8,128)(2,1)S(1)}, u32[]{:S(2)}, u32[]{:S(2)}) collective-permute-start(bf16[4,72,768]{2,1,0:T(8,128)(2,1)S(1)} %bitcast_dynamic-update-slice_fusion.8), channel_id=1, source_target_pairs={{0,16},{8,24},{16,0},{24,8},{1,17},{9,25},{17,1},{25,9},{2,18},{10... | collective-permute-start | bytes 1327112 | tf_op jit(solution)/shard_map/ppermute | solution.py:56
  80.6 21.4 %collective-permute-start.19 = (bf16[4,4,72,640]{3,2,1,0:T(8,128)(2,1)S(1)}, bf16[4,4,72,640]{3,2,1,0:T(8,128)(2,1)}, u32[]{:S(2)}, u32[]{:S(2)}) collective-permute-start(bf16[4,4,72,640]{3,2,1,0:T(8,128)(2,1)S(1)} %bitcast_dynamic-update-slice_fusion.4), channel_id=1, source_target_pairs={{0,4},{4,0},{1,5},{5,1},{2,6},{6,2},{3,7},{7,3},{8,12},{12,8},{9,1... | collective-permute-start | bytes 4423688 | tf_op jit(solution)/shard_map/ppermute | solution.py:56
  85.8 24.2 %collective-permute-start.23 = (bf16[4,4,72,768]{3,2,1,0:T(8,128)(2,1)S(1)}, bf16[4,4,72,768]{3,2,1,0:T(8,128)(2,1)}, u32[]{:S(2)}, u32[]{:S(2)}) collective-permute-start(bf16[4,4,72,768]{3,2,1,0:T(8,128)(2,1)S(1)} %bitcast_dynamic-update-slice_fusion.3), channel_id=1, source_target_pairs={{0,4},{4,0},{1,5},{5,1},{2,6},{6,2},{3,7},{7,3},{8,12},{12,8},{9,1... | collective-permute-start | bytes 5308424 | tf_op jit(solution)/shard_map/ppermute | solution.py:56
  133.8 16.0 %collective-permute-start.29 = (bf16[128,1152]{1,0:T(8,128)(2,1)S(1)}, bf16[128,1152]{1,0:T(8,128)(2,1)S(1)}, u32[]{:S(2)}, u32[]{:S(2)}) collective-permute-start(bf16[128,1152]{1,0:T(8,128)(2,1)S(1)} %get-tuple-element.57), channel_id=1, source_target_pairs={{0,1},{1,2},{2,3},{3,0},{4,5},{5,6},{6,7},{7,4},{8,9},{9,10},{10,1... | collective-permute-start | bytes 884744 | tf_op jit(solution)/shard_map/ppermute | solution.py:51
  149.8 14.9 %collective-permute-start.30 = (bf16[512,1152]{1,0:T(8,128)(2,1)S(1)}, bf16[512,1152]{1,0:T(8,128)(2,1)S(1)}, u32[]{:S(2)}, u32[]{:S(2)}) collective-permute-start(bf16[512,1152]{1,0:T(8,128)(2,1)S(1)} %pad_maximum_fusion.8), channel_id=1, source_target_pairs={{0,4},{4,0},{1,5},{5,1},{2,6},{6,2},{3,7},{7,3},{8,12},{12,8},{9,1... | collective-permute-start | bytes 3538952 | tf_op jit(solution)/shard_map/ppermute | solution.py:51
  188.4 16.0 %collective-permute-start.32 = (bf16[128,1152]{1,0:T(8,128)(2,1)S(1)}, bf16[128,1152]{1,0:T(8,128)(2,1)S(1)}, u32[]{:S(2)}, u32[]{:S(2)}) collective-permute-start(bf16[128,1152]{1,0:T(8,128)(2,1)S(1)} %get-tuple-element.83), channel_id=1, source_target_pairs={{0,1},{1,2},{2,3},{3,0},{4,5},{5,6},{6,7},{7,4},{8,9},{9,10},{10,1... | collective-permute-start | bytes 884744 | tf_op jit(solution)/shard_map/ppermute | solution.py:56
  209.0 16.0 %collective-permute-start.37 = (bf16[128,1152]{1,0:T(8,128)(2,1)S(1)}, bf16[128,1152]{1,0:T(8,128)(2,1)S(1)}, u32[]{:S(2)}, u32[]{:S(2)}) collective-permute-start(bf16[128,1152]{1,0:T(8,128)(2,1)S(1)} %get-tuple-element.53), channel_id=1, source_target_pairs={{0,1},{1,2},{2,3},{3,0},{4,5},{5,6},{6,7},{7,4},{8,9},{9,10},{10,1... | collective-permute-start | bytes 884744 | tf_op jit(solution)/shard_map/ppermute | solution.py:51
  260.3 16.6 %collective-permute-start.40 = (bf16[128,1152]{1,0:T(8,128)(2,1)S(1)}, bf16[128,1152]{1,0:T(8,128)(2,1)}, u32[]{:S(2)}, u32[]{:S(2)}) collective-permute-start(bf16[128,1152]{1,0:T(8,128)(2,1)S(1)} %get-tuple-element.80), channel_id=1, source_target_pairs={{0,1},{1,2},{2,3},{3,0},{4,5},{5,6},{6,7},{7,4},{8,9},{9,10},{10,1... | collective-permute-start | bytes 884744 | tf_op jit(solution)/shard_map/ppermute | solution.py:56
  327.9 15.4 %collective-permute-start.51 = (bf16[4,72,768]{2,1,0:T(8,128)(2,1)}, bf16[4,72,768]{2,1,0:T(8,128)(2,1)S(1)}, u32[]{:S(2)}, u32[]{:S(2)}) collective-permute-start(bf16[4,72,768]{2,1,0:T(8,128)(2,1)} %get-tuple-element.72), channel_id=1, source_target_pairs={{0,64},{32,96},{64,0},{96,32},{1,65},{33,97},{65,1},{97,33},{2,66}... | collective-permute-start | bytes 1327112 | tf_op jit(solution)/shard_map/ppermute | solution.py:56
  332.4 24.3 %collective-permute-start.50 = (bf16[4,72,768]{2,1,0:T(8,128)(2,1)S(1)}, bf16[4,72,768]{2,1,0:T(8,128)(2,1)S(1)}, u32[]{:S(2)}, u32[]{:S(2)}) collective-permute-start(bf16[4,72,768]{2,1,0:T(8,128)(2,1)S(1)} %get-tuple-element.70), channel_id=1, source_target_pairs={{0,32},{32,64},{64,96},{96,0},{1,33},{33,65},{65,97},{97,1},{2,34}... | collective-permute-start | bytes 1327112 | tf_op jit(solution)/shard_map/ppermute | solution.py:56
  334.9 23.3 %collective-permute-start.49 = (bf16[4,72,640]{2,1,0:T(8,128)(2,1)S(1)}, bf16[4,72,640]{2,1,0:T(8,128)(2,1)S(1)}, u32[]{:S(2)}, u32[]{:S(2)}) collective-permute-start(bf16[4,72,640]{2,1,0:T(8,128)(2,1)S(1)} %get-tuple-element.75), channel_id=1, source_target_pairs={{0,24},{8,0},{16,8},{24,16},{1,25},{9,1},{17,9},{25,17},{2,26},{10... | collective-permute-start | bytes 1105928 | tf_op jit(solution)/shard_map/ppermute | solution.py:56
  335.6 23.3 %collective-permute-start.48 = (bf16[4,72,640]{2,1,0:T(8,128)(2,1)S(1)}, bf16[4,72,640]{2,1,0:T(8,128)(2,1)S(1)}, u32[]{:S(2)}, u32[]{:S(2)}) collective-permute-start(bf16[4,72,640]{2,1,0:T(8,128)(2,1)S(1)} %get-tuple-element.74), channel_id=1, source_target_pairs={{0,16},{8,24},{16,0},{24,8},{1,17},{9,25},{17,1},{25,9},{2,18},{10... | collective-permute-start | bytes 1105928 | tf_op jit(solution)/shard_map/ppermute | solution.py:56
  340.3 20.7 %collective-permute-start.47 = (bf16[4,72,640]{2,1,0:T(8,128)(2,1)S(1)}, bf16[4,72,640]{2,1,0:T(8,128)(2,1)S(1)}, u32[]{:S(2)}, u32[]{:S(2)}) collective-permute-start(bf16[4,72,640]{2,1,0:T(8,128)(2,1)S(1)} %get-tuple-element.73), channel_id=1, source_target_pairs={{0,8},{8,16},{16,24},{24,0},{1,9},{9,17},{17,25},{25,1},{2,10},{10... | collective-permute-start | bytes 1105928 | tf_op jit(solution)/shard_map/ppermute | solution.py:56
  369.0 16.0 %collective-permute-start.59 = (bf16[56,1152]{1,0:T(8,128)(2,1)S(1)}, bf16[56,1152]{1,0:T(8,128)(2,1)S(1)}, u32[]{:S(2)}, u32[]{:S(2)}) collective-permute-start(bf16[56,1152]{1,0:T(8,128)(2,1)S(1)} %slice.341), channel_id=1, source_target_pairs={{0,1},{8,2},{16,3},{24,4},{32,5},{40,6},{48,7},{56,8},{64,9},{72,1... | collective-permute-start | bytes 387080 | tf_op jit(solution)/shard_map/ppermute | solution.py:452
  (122 other events, 932.1 us)
Sparse Core Ops, SparseCore 0:
  39.7 78.4 all-gather.1
  264.3 99.1 reduce-scatter.3
